TPU v7x, 256 devices: a whole 4x4x8 slice. The times are simulated.
256 devices in a mesh: tm: 128 (over y_lo, z, x, core), mode: 2 (over y_hi).
Axes of the slice: x: 4, y: 4 (y_hi: 2, y_lo: 2; y = y_hi * 2 + y_lo), z: 8, core: 2. Of those that a mesh axis runs over, the one named last changes fastest.
Arguments:
- elementals: bfloat16 [128, 128, 128, 128], P('tm', 'mode'), may hold values from -6 to 6
- slice_scale: float32 [128], P('tm'), may hold values from 0.5 to 2
- source_times: int32 [512, 1], replicated, may hold values from 0 to 127; in each aligned block of 512 rows (0 to 511, 512 to 1023, ...) at most 8 rows name the same one
- perambulators: bfloat16 [128, 8, 2, 128, 128], P('tm'), may hold values from -0.5 to 0.5
Outputs:
- correlator: float32 [128, 8, 2], P('tm')
Inputs may be any that keep to these rules, and one draw needn't show every extreme that they name: `source_times`: each of the 512 entries is a source time; no time is listed more than 8 times and some time is listed exactly 8 times; every time is listed at least once.
All inputs are finite; a program needn't handle non-finite values.
Results may differ from a plain program's by a relative error of at most 0.011.
Values may be sent and summed in bfloat16 or wider, within the bound.
A program may use at most 64 MiB of HBM per device.

v0:
```python
import functools
import math

import jax
import jax.numpy as jnp
from jax import lax
from jax.experimental import pallas as pl
from jax.experimental.pallas import tpu as pltpu
from jax.sharding import PartitionSpec as P

MESH = pl.DeviceIdType.MESH
F32, BF16 = jnp.float32, jnp.bfloat16
CHUNK = 16
PIECES = 2


def kernel(
    elem, scale, listed, peram, out,
    x_own, x_peer, x_rows, y_raw, y_cols, blocks, left, right, first, moved, acc,
    scale_own, scale_far, part, far,
    own_sem, peram_sem, x_send, x_recv, y_send, y_recv, p_send, p_recv, s_send, s_recv, o_send, o_recv,
):
    slices = lax.axis_size("tm")
    t, h = lax.axis_index("tm"), lax.axis_index("mode")
    core = lax.rem(t, 2)
    half, modes = elem.shape[1], elem.shape[2]
    slots = peram.shape[1]
    chunks, span = modes // CHUNK, half // PIECES
    other = 1 - h

    def at(step):
        return lax.rem(t + step + slices, slices)

    def send(src, dst, ssem, rsem, device):
        return pltpu.make_async_remote_copy(
            src_ref=src, dst_ref=dst, send_sem=ssem, recv_sem=rsem, device_id=device, device_id_type=MESH
        )

    def x_copy(i):
        rows = pl.ds(i * CHUNK, CHUNK)
        return send(elem.at[0, :, rows, :], x_peer.at[i], x_send.at[i], x_recv.at[i], (t, other))

    def y_copy(j, q, device):
        rows = pl.ds(q * span, span)
        return send(elem.at[0, rows], y_raw.at[j, rows], y_send.at[j, q], y_recv.at[j, q], device)

    def forward(q):
        rows = pl.ds(q * span, span)
        return send(y_raw.at[1, rows], y_raw.at[0, rows], y_send.at[0, q], y_recv.at[0, q], (at(1), h))

    def peram_copy():
        return send(peram.at[0, :, 1], blocks.at[1], p_send, p_recv, (at(2), h))

    def scale_copy(d):
        return send(scale_own, scale_far.at[d], s_send.at[d], s_recv.at[d], (at(-1 - d), h))

    own_copy = pltpu.make_async_copy(elem.at[0], x_own, own_sem)
    own_copy.start()
    block_copies = [pltpu.make_async_copy(peram.at[0, :, d], blocks.at[d], peram_sem.at[d]) for d in range(2)]
    block_copies[0].start()

    @pl.when(core == 0)
    def _():
        block_copies[1].start()

    scale_own[...] = jnp.full(scale_own.shape, scale[0], F32)
    acc[...] = jnp.zeros_like(acc)

    barrier = pltpu.get_barrier_semaphore()
    near = [(t, other)] + [(at(k), h) for k in (-2, -1, 1, 2)] + [(at(k), other) for k in (-2, 2)]
    for device in near:
        pl.semaphore_signal(barrier, inc=1, device_id=device, device_id_type=MESH)
    pl.semaphore_wait(barrier, len(near))

    @pl.when(core == 1)
    def _():
        peram_copy().start()
        for q in range(PIECES):
            y_copy(1, q, (at(2), h)).start()
            y_copy(0, q, (at(-1), h)).start()

    @pl.when(core == 0)
    def _():
        for q in range(PIECES):
            y_copy(1, q, (at(-2), h)).start()

    for d in range(2):
        scale_copy(d).start()
    for i in range(chunks):
        x_copy(i).start()

    block_copies[0].wait()

    @pl.when(core == 0)
    def _():
        block_copies[1].wait()

    @pl.when(core == 1)
    def _():
        peram_copy().wait_recv()

    right[...] = jnp.zeros_like(right)
    own_rows = pl.multiple_of(h * half, half)
    for j in range(2):
        swap = (core == 1) & (j == 1)

        def lay_block(r, _):
            block = blocks[j, r]
            turned = block.T
            row_form = jnp.where(swap, turned, block) if j else block
            column_form = jnp.where(swap, block, turned) if j else turned
            blocks[j, r] = row_form
            for q in range(PIECES):
                rows = pl.ds(pl.multiple_of(j * slots * span + r * span, span), span)
                left[q, rows, :] = blocks[j, r, pl.ds(own_rows + q * span, span), :]
            right[j * slots + r, :modes, :modes] = column_form
            right[j * slots + r, modes:, modes:] = column_form
            return 0

        lax.fori_loop(0, slots, lay_block, 0)

    def lay_rows(chunk_rows, i, offset):
        turned = jnp.swapaxes(chunk_rows.astype(F32), 0, 1).astype(BF16)
        for p in range(CHUNK // 2):
            pair = jnp.concatenate([turned[p], turned[p + CHUNK // 2]], axis=1)
            x_rows[i * (CHUNK // 2) + p, pl.ds(offset, half), :] = pair

    own_copy.wait()

    def lay_own(i, _):
        rows = pl.ds(pl.multiple_of(i * CHUNK, CHUNK), CHUNK)
        lay_rows(x_own[:, rows, :], i, own_rows)
        return 0

    lax.fori_loop(0, chunks, lay_own, 0)

    def take_piece(q):
        @pl.when(core == 0)
        def _():
            y_copy(1, q, (at(2), h)).wait_recv()
            forward(q).start()
            y_copy(0, q, (at(-1), h)).wait_recv()

        @pl.when(core == 1)
        def _():
            y_copy(1, q, (at(2), h)).wait_recv()
            forward(q).wait_recv()

        def lay(n, _):
            j, y = n // span, lax.rem(n, span)
            rows = pl.ds(pl.multiple_of(y * modes, modes), modes)
            y_cols[j, q, rows, :] = y_raw[j, q * span + y].T
            return 0

        lax.fori_loop(0, 2 * span, lay, 0)

    early = chunks // 2

    def unit(n, _):
        late = n - 2 * early
        i = jnp.where(n < 2 * early, lax.rem(n, early), early + late // 2)
        q = jnp.where(n < 2 * early, n // early, lax.rem(late, 2))

        @pl.when(n == 0)
        def _():
            take_piece(0)

        @pl.when(n == early)
        def _():
            take_piece(1)

        @pl.when((n < early) | ((late >= 0) & (q == 0)))
        def _():
            x_copy(i).wait_recv()
            lay_rows(x_peer[i], i, pl.multiple_of(other * half, half))

        for p in range(CHUNK // 2):
            product = jnp.dot(left[q], x_rows[i * (CHUNK // 2) + p], preferred_element_type=F32)
            first[p] = product.astype(BF16)
        for j in range(2):
            for r in range(slots):
                lo = (j * slots + r) * span
                lhs = first[:, lo:lo + span, :].reshape(CHUNK // 2 * span, 2 * modes)
                image = jnp.dot(lhs, right[j * slots + r], preferred_element_type=F32)
                turned = jnp.swapaxes(image.reshape(CHUNK // 2, span, 2 * modes), 0, 1)
                for y in range(span):
                    tile = jnp.concatenate([turned[y, :, :modes], turned[y, :, modes:]], axis=0)
                    moved[j, r * CHUNK:(r + 1) * CHUNK, y * modes:(y + 1) * modes] = tile.astype(BF16)
        rows = pl.ds(pl.multiple_of(i * CHUNK, CHUNK), CHUNK)
        for j in range(2):
            sums = jnp.dot(moved[j], y_cols[j, q], preferred_element_type=F32)
            weights = right[pl.ds(j * slots, slots), rows, :modes].reshape(slots * CHUNK, modes)
            acc[j] += sums * weights.astype(F32)
        return 0

    lax.fori_loop(0, 2 * chunks, unit, 0)

    for j in range(2):
        total = jnp.sum(acc[j].reshape(slots, CHUNK, modes), axis=1)
        part[j] = jnp.broadcast_to(jnp.sum(total, axis=1, keepdims=True), (slots, modes))

    def part_copy(j, slot, device):
        return send(part.at[j], far.at[slot], o_send.at[slot], o_recv.at[slot], device)

    part_copy(0, 0, (t, other)).start()

    @pl.when(core == 0)
    def _():
        part_copy(1, 2, (t, other)).start()
        far[1] = part[1]

    @pl.when(core == 1)
    def _():
        part_copy(1, 1, (at(-2), h)).start()
        part_copy(1, 2, (at(-2), other)).start()

    live = jnp.sum((listed[...] == t).astype(jnp.int32))
    slot_of = lax.broadcasted_iota(jnp.int32, (slots, modes), 0)
    lane = lax.broadcasted_iota(jnp.int32, (slots, modes), 1)
    for d in range(2):
        scale_copy(d).wait_recv()
    factor = 1.0 / (modes * math.sqrt(modes))
    signs = [jnp.where(t + d >= slices, -factor, factor) for d in (1, 2)]
    weights = jnp.where(lane == 0, scale_far[0] * signs[0], scale_far[1] * signs[1]) * scale_own[...]

    part_copy(0, 0, (t, other)).wait_recv()
    part_copy(1, 2, (t, other)).wait_recv()

    @pl.when(core == 1)
    def _():
        part_copy(1, 1, (at(-2), h)).wait_recv()

    values = jnp.where(lane == 0, part[0] + far[0], far[1] + far[2]) * weights
    values = jnp.where(slot_of < live, values, 0.0)
    out[0] = values[:, :2]

    part_copy(0, 0, (t, other)).wait_send()
    part_copy(1, 2, (t, other)).wait_send()

    @pl.when(core == 0)
    def _():
        for q in range(PIECES):
            y_copy(1, q, (at(-2), h)).wait_send()
            forward(q).wait_send()

    @pl.when(core == 1)
    def _():
        peram_copy().wait_send()
        part_copy(1, 1, (at(-2), h)).wait_send()
        for q in range(PIECES):
            y_copy(1, q, (at(2), h)).wait_send()
            y_copy(0, q, (at(-1), h)).wait_send()

    for d in range(2):
        scale_copy(d).wait_send()
    for i in range(chunks):
        x_copy(i).wait_send()


def local(elementals, slice_scale, source_times, perambulators):
    half, modes = elementals.shape[1:3]
    slots = perambulators.shape[1]
    chunks, span = modes // CHUNK, half // PIECES
    dma, in_hbm = pltpu.SemaphoreType.DMA, pl.BlockSpec(memory_space=pltpu.HBM)
    return pl.pallas_call(
        kernel,
        out_shape=jax.ShapeDtypeStruct((1, slots, 2), F32),
        in_specs=[
            in_hbm,
            pl.BlockSpec(memory_space=pltpu.SMEM),
            pl.BlockSpec(memory_space=pltpu.VMEM),
            in_hbm,
        ],
        out_specs=pl.BlockSpec(memory_space=pltpu.VMEM),
        scratch_shapes=[
            pltpu.VMEM((half, modes, modes), BF16),
            pltpu.VMEM((chunks, half, CHUNK, modes), BF16),
            pltpu.VMEM((modes // 2, 2 * half, 2 * modes), BF16),
            pltpu.VMEM((2, half, modes, modes), BF16),
            pltpu.VMEM((2, PIECES, span * modes, modes), BF16),
            pltpu.VMEM((2, slots, modes, modes), BF16),
            pltpu.VMEM((PIECES, 2 * slots * span, modes), BF16),
            pltpu.VMEM((2 * slots, 2 * modes, 2 * modes), BF16),
            pltpu.VMEM((CHUNK // 2, 2 * slots * span, 2 * modes), BF16),
            pltpu.VMEM((2, slots * CHUNK, span * modes), BF16),
            pltpu.VMEM((2, slots * CHUNK, modes), F32),
            pltpu.VMEM((slots, modes), F32),
            pltpu.VMEM((2, slots, modes), F32),
            pltpu.VMEM((2, slots, modes), F32),
            pltpu.VMEM((3, slots, modes), F32),
            dma, dma((2,)),
            dma((chunks,)), dma((chunks,)),
            dma((2, PIECES)), dma((2, PIECES)),
            dma, dma,
            dma((2,)), dma((2,)),
            dma((3,)), dma((3,)),
        ],
        compiler_params=pltpu.CompilerParams(
            collective_id=0, has_side_effects=True, vmem_limit_bytes=48 * 2**20
        ),
    )(elementals, slice_scale, source_times.T, perambulators)


def solution(mesh):
    in_specs = (P("tm", "mode", None, None), P("tm"), P(), P("tm", None, None, None, None))
    return jax.shard_map(
        local, mesh=mesh, in_specs=in_specs, out_specs=P("tm", None, None), check_vma=False
    )
```

profile of v0, /device:TPU:1, one launch (start us, length us, event | category | flops | bytes accessed | tf_op | source)
XLA Modules:
  0.0 104.2 jit_solution(1006311955411594231)
XLA Ops:
  0.7 0.0 copy-start
  0.7 1.6 %copy-done = bf16[1,64,128,128]{3,2,1,0:T(8,128)(2,1)S(1)} copy-done((bf16[1,64,128,128]{3,2,1,0:T(8,128)(2,1)S(1)}, bf16[1,64,128,128]{3,2,1,0:T(8,128)(2,1)}, u32[]{:S(2)}) %copy-start) | copy-done | bytes 2097176
  2.2 0.0 copy-start.1
  2.2 1.0 copy-done.1
  3.3 0.0 copy-start.2
  3.3 0.7 copy-done.2
  4.0 99.6 %shard_map.46 = f32[1,8,2]{2,1,0:T(8,128)S(1)} custom-call(bf16[1,64,128,128]{3,2,1,0:T(8,128)(2,1)S(1)} %copy-done, f32[1]{0:T(128)S(6)} %copy.6.scale, s32[1,512]{1,0:T(1,128)S(1)} %bitcast.1, bf16[1,8,2,128,128]{4,3,2,1,0:T(8,128)(2,1)S(1)} %copy-done.1), custom_call_target="tpu_custom_call" | custom-call | tf_op jit(solution)/shard_map/pallas_call | solution.py:265
  103.5 0.6 copy.5
Async XLA Ops:
  0.7 1.6 %copy-start = (bf16[1,64,128,128]{3,2,1,0:T(8,128)(2,1)S(1)}, bf16[1,64,128,128]{3,2,1,0:T(8,128)(2,1)}, u32[]{:S(2)}) copy-start(bf16[1,64,128,128]{3,2,1,0:T(8,128)(2,1)} %elem.1) | copy-start | bytes 6291460
  2.2 1.0 copy-start.1
  3.3 0.7 copy-start.2
where the time goes:
time: 104 us
  Pallas kernels  99.6 us (96%)
  local copies, waits for them, and re-layouts  3.94 us (4%)
    pallas_call x1, Pallas kernels, local(): pl.pallas_call(kernel, out_shape=jax.ShapeDtypeStruct((1, slots, 2), F32)...  99.6 us
    unnamed x6, local copies, waits for them, and re-layouts  3.31 us

commit v1 on v0

--- a/solution.py
+++ b/solution.py
@@ -12,13 +12,14 @@
 F32, BF16 = jnp.float32, jnp.bfloat16
 CHUNK = 16
 PIECES = 2
+STRIDE = 8
 
 
 def kernel(
     elem, scale, listed, peram, out,
-    x_own, x_peer, x_rows, y_raw, y_cols, blocks, left, right, first, moved, acc,
-    scale_own, scale_far, part, far,
-    own_sem, peram_sem, x_send, x_recv, y_send, y_recv, p_send, p_recv, s_send, s_recv, o_send, o_recv,
+    x_own, x_peer, x_rows, y_raw, blocks, left, right, first, moved, acc,
+    scale_own, scale_far, part, far, passing,
+    own_sem, peram_sem, x_send, x_recv, y_send, y_recv, p_send, p_recv, s_send, s_recv, o_send, o_recv, r_send, r_recv,
 ):
     slices = lax.axis_size("tm")
     t, h = lax.axis_index("tm"), lax.axis_index("mode")
@@ -54,6 +55,28 @@
     def scale_copy(d):
         return send(scale_own, scale_far.at[d], s_send.at[d], s_recv.at[d], (at(-1 - d), h))
 
+    run = slices // 2
+    place, upper = lax.rem(t, run), t // run
+    relays = run // STRIDE
+    share = span // relays
+    rank = place // STRIDE
+    lead = jnp.where(core == 1, 1, STRIDE - 2)
+    at_source = place == jnp.where(core == 1, run - 1, 0)
+    at_sink = place == jnp.where(core == 1, 1, run - 2)
+    is_relay = (lax.rem(place, STRIDE) == lead) & jnp.logical_not(at_sink)
+    sink = upper * run + jnp.where(core == 1, 1, run - 2)
+    source = lax.rem(sink + jnp.where(core == 1, slices - 2, 2), slices)
+    ahead = lax.rem(t + jnp.where(core == 1, 2, slices - 2), slices)
+
+    def share_rows(q, k):
+        return pl.ds(q * span + k * share, share)
+
+    def share_copy(q, k, dst, rsem, device):
+        return send(elem.at[0, share_rows(q, k)], dst, y_send.at[1, q], rsem, device)
+
+    def pass_on(q):
+        return send(passing.at[q], y_raw.at[1, share_rows(q, rank)], r_send.at[q], y_recv.at[1, q], (sink, h))
+
     own_copy = pltpu.make_async_copy(elem.at[0], x_own, own_sem)
     own_copy.start()
     block_copies = [pltpu.make_async_copy(peram.at[0, :, d], blocks.at[d], peram_sem.at[d]) for d in range(2)]
@@ -70,38 +93,67 @@
     near = [(t, other)] + [(at(k), h) for k in (-2, -1, 1, 2)] + [(at(k), other) for k in (-2, 2)]
     for device in near:
         pl.semaphore_signal(barrier, inc=1, device_id=device, device_id_type=MESH)
-    pl.semaphore_wait(barrier, len(near))
+
+    @pl.when(is_relay)
+    def _():
+        pl.semaphore_signal(barrier, inc=1, device_id=(source, h), device_id_type=MESH)
+
+    @pl.when(at_sink)
+    def _():
+        def greet(k, _):
+            @pl.when(k != rank)
+            def _():
+                relay = upper * run + k * STRIDE + lead
+                pl.semaphore_signal(barrier, inc=1, device_id=(relay, h), device_id_type=MESH)
+
+            return 0
+
+        lax.fori_loop(0, relays, greet, 0)
+
+    further = jnp.where(is_relay, 1, 0) + jnp.where(at_source, relays - 1, 0)
+    pl.semaphore_wait(barrier, len(near) + further)
 
     @pl.when(core == 1)
     def _():
         peram_copy().start()
-        for q in range(PIECES):
-            y_copy(1, q, (at(2), h)).start()
+
+    @pl.when(at_source)
+    def _():
+        def spread(n, _):
+            q, k = n // relays, lax.rem(n, relays)
+            relay = (1 - upper) * run + k * STRIDE + lead
+
+            @pl.when(relay == ahead)
+            def _():
+                share_copy(q, k, y_raw.at[1, share_rows(q, k)], y_recv.at[1, q], (relay, h)).start()
+
+            @pl.when(relay != ahead)
+            def _():
+                share_copy(q, k, passing.at[q], r_recv.at[q], (relay, h)).start()
+
+            return 0
+
+        lax.fori_loop(0, PIECES * relays, spread, 0)
+
+    @pl.when(jnp.logical_not(at_source))
+    def _():
+        for q in range(PIECES):
+            y_copy(1, q, (ahead, h)).start()
+
+    @pl.when(core == 1)
+    def _():
+        for q in range(PIECES):
             y_copy(0, q, (at(-1), h)).start()
-
-    @pl.when(core == 0)
-    def _():
-        for q in range(PIECES):
-            y_copy(1, q, (at(-2), h)).start()
 
     for d in range(2):
         scale_copy(d).start()
     for i in range(chunks):
         x_copy(i).start()
 
-    block_copies[0].wait()
-
-    @pl.when(core == 0)
-    def _():
-        block_copies[1].wait()
-
-    @pl.when(core == 1)
-    def _():
-        peram_copy().wait_recv()
-
     right[...] = jnp.zeros_like(right)
     own_rows = pl.multiple_of(h * half, half)
-    for j in range(2):
+
+    def lay_blocks(j):
         swap = (core == 1) & (j == 1)
 
         def lay_block(r, _):
@@ -111,8 +163,8 @@
             column_form = jnp.where(swap, block, turned) if j else turned
             blocks[j, r] = row_form
             for q in range(PIECES):
-                rows = pl.ds(pl.multiple_of(j * slots * span + r * span, span), span)
-                left[q, rows, :] = blocks[j, r, pl.ds(own_rows + q * span, span), :]
+                rows = pl.ds(pl.multiple_of(r * span, span), span)
+                left[j, q, rows, :] = blocks[j, r, pl.ds(own_rows + q * span, span), :]
             right[j * slots + r, :modes, :modes] = column_form
             right[j * slots + r, modes:, modes:] = column_form
             return 0
@@ -125,34 +177,39 @@
             pair = jnp.concatenate([turned[p], turned[p + CHUNK // 2]], axis=1)
             x_rows[i * (CHUNK // 2) + p, pl.ds(offset, half), :] = pair
 
-    own_copy.wait()
-
     def lay_own(i, _):
         rows = pl.ds(pl.multiple_of(i * CHUNK, CHUNK), CHUNK)
         lay_rows(x_own[:, rows, :], i, own_rows)
         return 0
 
+    block_copies[0].wait()
+    lay_blocks(0)
+    own_copy.wait()
     lax.fori_loop(0, chunks, lay_own, 0)
 
-    def take_piece(q):
+    @pl.when(core == 0)
+    def _():
+        block_copies[1].wait()
+
+    @pl.when(core == 1)
+    def _():
+        peram_copy().wait_recv()
+
+    lay_blocks(1)
+
+    def take(q):
+        y_copy(1, q, (at(2), h)).wait_recv()
+
         @pl.when(core == 0)
         def _():
-            y_copy(1, q, (at(2), h)).wait_recv()
             forward(q).start()
-            y_copy(0, q, (at(-1), h)).wait_recv()
-
-        @pl.when(core == 1)
+
+        @pl.when(is_relay)
         def _():
-            y_copy(1, q, (at(2), h)).wait_recv()
-            forward(q).wait_recv()
-
-        def lay(n, _):
-            j, y = n // span, lax.rem(n, span)
-            rows = pl.ds(pl.multiple_of(y * modes, modes), modes)
-            y_cols[j, q, rows, :] = y_raw[j, q * span + y].T
-            return 0
-
-        lax.fori_loop(0, 2 * span, lay, 0)
+            share_copy(q, 0, passing.at[q], r_recv.at[q], (source, h)).wait_recv()
+            pass_on(q).start()
+
+        y_copy(0, q, (at(-1), h)).wait_recv()
 
     early = chunks // 2
 
@@ -161,26 +218,23 @@
         i = jnp.where(n < 2 * early, lax.rem(n, early), early + late // 2)
         q = jnp.where(n < 2 * early, n // early, lax.rem(late, 2))
 
-        @pl.when(n == 0)
-        def _():
-            take_piece(0)
-
-        @pl.when(n == early)
-        def _():
-            take_piece(1)
+        for piece in range(PIECES):
+            @pl.when(n == piece * early)
+            def _():
+                take(piece)
 
         @pl.when((n < early) | ((late >= 0) & (q == 0)))
         def _():
             x_copy(i).wait_recv()
             lay_rows(x_peer[i], i, pl.multiple_of(other * half, half))
 
-        for p in range(CHUNK // 2):
-            product = jnp.dot(left[q], x_rows[i * (CHUNK // 2) + p], preferred_element_type=F32)
-            first[p] = product.astype(BF16)
+        for j in range(2):
+            for p in range(CHUNK // 2):
+                product = jnp.dot(left[j, q], x_rows[i * (CHUNK // 2) + p], preferred_element_type=F32)
+                first[j, p] = product.astype(BF16)
         for j in range(2):
             for r in range(slots):
-                lo = (j * slots + r) * span
-                lhs = first[:, lo:lo + span, :].reshape(CHUNK // 2 * span, 2 * modes)
+                lhs = first[j, :, r * span:(r + 1) * span, :].reshape(CHUNK // 2 * span, 2 * modes)
                 image = jnp.dot(lhs, right[j * slots + r], preferred_element_type=F32)
                 turned = jnp.swapaxes(image.reshape(CHUNK // 2, span, 2 * modes), 0, 1)
                 for y in range(span):
@@ -188,8 +242,9 @@
                     moved[j, r * CHUNK:(r + 1) * CHUNK, y * modes:(y + 1) * modes] = tile.astype(BF16)
         rows = pl.ds(pl.multiple_of(i * CHUNK, CHUNK), CHUNK)
         for j in range(2):
-            sums = jnp.dot(moved[j], y_cols[j, q], preferred_element_type=F32)
-            weights = right[pl.ds(j * slots, slots), rows, :modes].reshape(slots * CHUNK, modes)
+            sink_rows = jnp.concatenate([y_raw[j, q * span + y] for y in range(span)], axis=1)
+            sums = lax.dot_general(moved[j], sink_rows, (((1,), (1,)), ((), ())), preferred_element_type=F32)
+            weights = right[j * slots:(j + 1) * slots, rows, :modes].reshape(slots * CHUNK, modes)
             acc[j] += sums * weights.astype(F32)
         return 0
 
@@ -237,10 +292,12 @@
     part_copy(0, 0, (t, other)).wait_send()
     part_copy(1, 2, (t, other)).wait_send()
 
+    for q in range(PIECES):
+        y_copy(1, q, (ahead, h)).wait_send()
+
     @pl.when(core == 0)
     def _():
         for q in range(PIECES):
-            y_copy(1, q, (at(-2), h)).wait_send()
             forward(q).wait_send()
 
     @pl.when(core == 1)
@@ -248,8 +305,12 @@
         peram_copy().wait_send()
         part_copy(1, 1, (at(-2), h)).wait_send()
         for q in range(PIECES):
-            y_copy(1, q, (at(2), h)).wait_send()
             y_copy(0, q, (at(-1), h)).wait_send()
+
+    @pl.when(is_relay)
+    def _():
+        for q in range(PIECES):
+            pass_on(q).wait_send()
 
     for d in range(2):
         scale_copy(d).wait_send()
@@ -277,26 +338,27 @@
             pltpu.VMEM((chunks, half, CHUNK, modes), BF16),
             pltpu.VMEM((modes // 2, 2 * half, 2 * modes), BF16),
             pltpu.VMEM((2, half, modes, modes), BF16),
-            pltpu.VMEM((2, PIECES, span * modes, modes), BF16),
             pltpu.VMEM((2, slots, modes, modes), BF16),
-            pltpu.VMEM((PIECES, 2 * slots * span, modes), BF16),
+            pltpu.VMEM((2, PIECES, slots * span, modes), BF16),
             pltpu.VMEM((2 * slots, 2 * modes, 2 * modes), BF16),
-            pltpu.VMEM((CHUNK // 2, 2 * slots * span, 2 * modes), BF16),
+            pltpu.VMEM((2, CHUNK // 2, slots * span, 2 * modes), BF16),
             pltpu.VMEM((2, slots * CHUNK, span * modes), BF16),
             pltpu.VMEM((2, slots * CHUNK, modes), F32),
             pltpu.VMEM((slots, modes), F32),
             pltpu.VMEM((2, slots, modes), F32),
             pltpu.VMEM((2, slots, modes), F32),
             pltpu.VMEM((3, slots, modes), F32),
+            pltpu.VMEM((PIECES, span * STRIDE * 2 // lax.axis_size("tm"), modes, modes), BF16),
             dma, dma((2,)),
             dma((chunks,)), dma((chunks,)),
             dma((2, PIECES)), dma((2, PIECES)),
             dma, dma,
             dma((2,)), dma((2,)),
             dma((3,)), dma((3,)),
+            dma((PIECES,)), dma((PIECES,)),
         ],
         compiler_params=pltpu.CompilerParams(
-            collective_id=0, has_side_effects=True, vmem_limit_bytes=48 * 2**20
+            collective_id=0, has_side_effects=True, vmem_limit_bytes=60 * 2**20
         ),
     )(elementals, slice_scale, source_times.T, perambulators)
 

time: 104 us -> 83.7 us (0.80)
  Pallas kernels: 99.6 us -> 81.6 us
  local copies, waits for them, and re-layouts: 3.94 us -> 1.32 us
    pallas_call x1, Pallas kernels: 99.6 us -> 81.6 us  [local(): pl.pallas_call(kernel, out_shape=jax.ShapeDtypeStruct((1, slots, 2), F32)...]
    unnamed x6 -> x0, local copies, waits for them, and re-layouts: 3.31 us -> none
where the time goes in v1:
time: 83.7 us; the launch traced here: 83.5 us
  Pallas kernels  81.6 us (97%)
  local copies, waits for them, and re-layouts  1.32 us (2%)
    pallas_call x1, Pallas kernels, local(): pl.pallas_call(kernel, out_shape=jax.ShapeDtypeStruct((1, slots, 2), F32)...  81.6 us

profile of v1, /device:TPU:1, one launch (start us, length us, event | category | flops | bytes accessed | tf_op | source)
XLA Modules:
  0.0 83.5 jit_solution(17757940389930599465)
XLA Ops:
  0.7 81.6 %shard_map.46 = f32[1,8,2]{2,1,0:T(8,128)} custom-call(bf16[1,64,128,128]{3,2,1,0:T(8,128)(2,1)} %elem.1, f32[1]{0:T(128)S(6)} %copy.6.scale, s32[1,512]{1,0:T(1,128)} %bitcast.1, bf16[1,8,2,128,128]{4,3,2,1,0:T(8,128)(2,1)} %peram.1), custom_call_target="tpu_custom_call" | custom-call | tf_op jit(solution)/shard_map/pallas_call | solution.py:326
  82.2 1.3 %copy.5 = f32[1,8,2]{1,2,0:T(2,128)} copy(f32[1,8,2]{2,1,0:T(8,128)} %shard_map.46) | data formatting | bytes 128 | tf_op jit(solution)/shard_map/pallas_call | solution.py:326

commit v2 on v1

--- a/solution.py
+++ b/solution.py
@@ -60,10 +60,10 @@
     relays = run // STRIDE
     share = span // relays
     rank = place // STRIDE
-    lead = jnp.where(core == 1, 1, STRIDE - 2)
+    leads = [jnp.where(core == 1, 1 + 2 * q, STRIDE - 2 - 2 * q) for q in range(PIECES)]
     at_source = place == jnp.where(core == 1, run - 1, 0)
     at_sink = place == jnp.where(core == 1, 1, run - 2)
-    is_relay = (lax.rem(place, STRIDE) == lead) & jnp.logical_not(at_sink)
+    relays_piece = [(lax.rem(place, STRIDE) == lead) & jnp.logical_not(at_sink) for lead in leads]
     sink = upper * run + jnp.where(core == 1, 1, run - 2)
     source = lax.rem(sink + jnp.where(core == 1, slices - 2, 2), slices)
     ahead = lax.rem(t + jnp.where(core == 1, 2, slices - 2), slices)
@@ -94,24 +94,28 @@
     for device in near:
         pl.semaphore_signal(barrier, inc=1, device_id=device, device_id_type=MESH)
 
-    @pl.when(is_relay)
+    @pl.when(relays_piece[0] | relays_piece[1])
     def _():
         pl.semaphore_signal(barrier, inc=1, device_id=(source, h), device_id_type=MESH)
 
     @pl.when(at_sink)
     def _():
-        def greet(k, _):
-            @pl.when(k != rank)
+        def greet(n, _):
+            relay = upper * run + lax.rem(n, relays) * STRIDE + jnp.where(n < relays, leads[0], leads[1])
+
+            @pl.when(relay != t)
             def _():
-                relay = upper * run + k * STRIDE + lead
                 pl.semaphore_signal(barrier, inc=1, device_id=(relay, h), device_id_type=MESH)
 
             return 0
 
-        lax.fori_loop(0, relays, greet, 0)
-
-    further = jnp.where(is_relay, 1, 0) + jnp.where(at_source, relays - 1, 0)
+        lax.fori_loop(0, PIECES * relays, greet, 0)
+
+    further = jnp.where(relays_piece[0] | relays_piece[1], 1, 0) + jnp.where(at_source, PIECES * relays - 1, 0)
     pl.semaphore_wait(barrier, len(near) + further)
+
+    for i in range(2):
+        x_copy(i).start()
 
     @pl.when(core == 1)
     def _():
@@ -121,7 +125,7 @@
     def _():
         def spread(n, _):
             q, k = n // relays, lax.rem(n, relays)
-            relay = (1 - upper) * run + k * STRIDE + lead
+            relay = (1 - upper) * run + k * STRIDE + jnp.where(q == 0, leads[0], leads[1])
 
             @pl.when(relay == ahead)
             def _():
@@ -133,22 +137,27 @@
 
             return 0
 
-        lax.fori_loop(0, PIECES * relays, spread, 0)
+        group = relays // 2
+        for g in range(2 * PIECES):
+            lax.fori_loop(g * group, (g + 1) * group, spread, 0)
+            x_copy(2 + g).start()
 
     @pl.when(jnp.logical_not(at_source))
     def _():
         for q in range(PIECES):
             y_copy(1, q, (ahead, h)).start()
+        for g in range(2 * PIECES):
+            x_copy(2 + g).start()
 
     @pl.when(core == 1)
     def _():
         for q in range(PIECES):
             y_copy(0, q, (at(-1), h)).start()
 
+    for i in range(2 + 2 * PIECES, chunks):
+        x_copy(i).start()
     for d in range(2):
         scale_copy(d).start()
-    for i in range(chunks):
-        x_copy(i).start()
 
     right[...] = jnp.zeros_like(right)
     own_rows = pl.multiple_of(h * half, half)
@@ -197,58 +206,90 @@
 
     lay_blocks(1)
 
-    def take(q):
+    def take_near(q):
+        y_copy(0, q, (at(-1), h)).wait_recv()
+
+    def take_far(q):
         y_copy(1, q, (at(2), h)).wait_recv()
 
         @pl.when(core == 0)
         def _():
             forward(q).start()
 
-        @pl.when(is_relay)
+    def relay(q):
+        @pl.when(relays_piece[q])
         def _():
             share_copy(q, 0, passing.at[q], r_recv.at[q], (source, h)).wait_recv()
             pass_on(q).start()
 
-        y_copy(0, q, (at(-1), h)).wait_recv()
-
+    def take_chunk(i):
+        x_copy(i).wait_recv()
+        lay_rows(x_peer[i], i, pl.multiple_of(other * half, half))
+
+    near_late = (core == 1) & at_source
+    far_late = (core == 1) & at_sink
     early = chunks // 2
-
-    def unit(n, _):
-        late = n - 2 * early
-        i = jnp.where(n < 2 * early, lax.rem(n, early), early + late // 2)
-        q = jnp.where(n < 2 * early, n // early, lax.rem(late, 2))
-
-        for piece in range(PIECES):
-            @pl.when(n == piece * early)
-            def _():
-                take(piece)
-
-        @pl.when((n < early) | ((late >= 0) & (q == 0)))
-        def _():
-            x_copy(i).wait_recv()
-            lay_rows(x_peer[i], i, pl.multiple_of(other * half, half))
-
-        for j in range(2):
+    last = PIECES - 1
+
+    def step(n, _):
+        @pl.when(n == 0)
+        def _():
+            take_chunk(0)
+            relay(0)
+            take_far(0)
+            take_near(0)
+            take_chunk(1)
+
+        @pl.when(n == 1)
+        def _():
+            take_chunk(2)
+            relay(last)
+            take_chunk(3)
+
+        far_at = jnp.where(at_sink, jnp.where(core == 1, 3, 2), 1)
+
+        @pl.when(n == far_at)
+        def _():
+            take_far(last)
+
+        @pl.when(n == jnp.where(near_late, 3, 2))
+        def _():
+            take_near(last)
+
+        @pl.when(n >= early)
+        def _():
+            take_chunk(n)
+
+        pairs, apart = n < early, (near_late | far_late) & ((n == 2) | (n == 3))
+        late_first = (n == 2) == near_late
+        blocks_of = []
+        for b in range(4):
+            c = jnp.where(pairs, 2 * lax.rem(n, 2) + b // 2, n)
+            q = jnp.where(pairs, n // 2, b // 2)
+            c = jnp.where(apart, b, c)
+            j = jnp.where(apart, jnp.where(late_first, 1, 0), b % 2)
+            blocks_of.append((c, j, q))
+        for b, (c, j, q) in enumerate(blocks_of):
             for p in range(CHUNK // 2):
-                product = jnp.dot(left[j, q], x_rows[i * (CHUNK // 2) + p], preferred_element_type=F32)
-                first[j, p] = product.astype(BF16)
-        for j in range(2):
+                product = jnp.dot(left[j, q], x_rows[c * (CHUNK // 2) + p], preferred_element_type=F32)
+                first[b, p] = product.astype(BF16)
+        for b, (c, j, q) in enumerate(blocks_of):
             for r in range(slots):
-                lhs = first[j, :, r * span:(r + 1) * span, :].reshape(CHUNK // 2 * span, 2 * modes)
+                lhs = first[b, :, r * span:(r + 1) * span, :].reshape(CHUNK // 2 * span, 2 * modes)
                 image = jnp.dot(lhs, right[j * slots + r], preferred_element_type=F32)
                 turned = jnp.swapaxes(image.reshape(CHUNK // 2, span, 2 * modes), 0, 1)
                 for y in range(span):
                     tile = jnp.concatenate([turned[y, :, :modes], turned[y, :, modes:]], axis=0)
-                    moved[j, r * CHUNK:(r + 1) * CHUNK, y * modes:(y + 1) * modes] = tile.astype(BF16)
-        rows = pl.ds(pl.multiple_of(i * CHUNK, CHUNK), CHUNK)
-        for j in range(2):
+                    moved[b, r * CHUNK:(r + 1) * CHUNK, y * modes:(y + 1) * modes] = tile.astype(BF16)
+        for b, (c, j, q) in enumerate(blocks_of):
+            rows = pl.ds(pl.multiple_of(c * CHUNK, CHUNK), CHUNK)
             sink_rows = jnp.concatenate([y_raw[j, q * span + y] for y in range(span)], axis=1)
-            sums = lax.dot_general(moved[j], sink_rows, (((1,), (1,)), ((), ())), preferred_element_type=F32)
-            weights = right[j * slots:(j + 1) * slots, rows, :modes].reshape(slots * CHUNK, modes)
+            sums = lax.dot_general(moved[b], sink_rows, (((1,), (1,)), ((), ())), preferred_element_type=F32)
+            weights = right[pl.ds(j * slots, slots), rows, :modes].reshape(slots * CHUNK, modes)
             acc[j] += sums * weights.astype(F32)
         return 0
 
-    lax.fori_loop(0, 2 * chunks, unit, 0)
+    lax.fori_loop(0, chunks, step, 0)
 
     for j in range(2):
         total = jnp.sum(acc[j].reshape(slots, CHUNK, modes), axis=1)
@@ -307,9 +348,9 @@
         for q in range(PIECES):
             y_copy(0, q, (at(-1), h)).wait_send()
 
-    @pl.when(is_relay)
-    def _():
-        for q in range(PIECES):
+    for q in range(PIECES):
+        @pl.when(relays_piece[q])
+        def _():
             pass_on(q).wait_send()
 
     for d in range(2):
@@ -341,8 +382,8 @@
             pltpu.VMEM((2, slots, modes, modes), BF16),
             pltpu.VMEM((2, PIECES, slots * span, modes), BF16),
             pltpu.VMEM((2 * slots, 2 * modes, 2 * modes), BF16),
-            pltpu.VMEM((2, CHUNK // 2, slots * span, 2 * modes), BF16),
-            pltpu.VMEM((2, slots * CHUNK, span * modes), BF16),
+            pltpu.VMEM((4, CHUNK // 2, slots * span, 2 * modes), BF16),
+            pltpu.VMEM((4, slots * CHUNK, span * modes), BF16),
             pltpu.VMEM((2, slots * CHUNK, modes), F32),
             pltpu.VMEM((slots, modes), F32),
             pltpu.VMEM((2, slots, modes), F32),

time: 83.7 us -> 76.4 us (0.913)
  the two profiles are of different devices: /device:TPU:1 before, /device:TPU:229 now
where the time goes in v2:
time: 76.4 us; the launch traced here: 76.3 us
  Pallas kernels  74.3 us (97%)
  local copies, waits for them, and re-layouts  1.32 us (2%)
    pallas_call x1, Pallas kernels, local(): pl.pallas_call(kernel, out_shape=jax.ShapeDtypeStruct((1, slots, 2), F32)...  74.3 us

profile of v2, /device:TPU:229, one launch (start us, length us, event | category | flops | bytes accessed | tf_op | source)
XLA Modules:
  0.0 76.3 jit_solution(12300145780667620291)
XLA Ops:
  0.7 74.3 %shard_map.46 = f32[1,8,2]{2,1,0:T(8,128)} custom-call(bf16[1,64,128,128]{3,2,1,0:T(8,128)(2,1)} %elem.1, f32[1]{0:T(128)S(6)} %copy.6.scale, s32[1,512]{1,0:T(1,128)} %bitcast.1, bf16[1,8,2,128,128]{4,3,2,1,0:T(8,128)(2,1)} %peram.1), custom_call_target="tpu_custom_call" | custom-call | tf_op jit(solution)/shard_map/pallas_call | solution.py:367
  74.9 1.3 %copy.5 = f32[1,8,2]{1,2,0:T(2,128)} copy(f32[1,8,2]{2,1,0:T(8,128)} %shard_map.46) | data formatting | bytes 128 | tf_op jit(solution)/shard_map/pallas_call | solution.py:367

commit v3 on v2

--- a/solution.py
+++ b/solution.py
@@ -18,8 +18,8 @@
 def kernel(
     elem, scale, listed, peram, out,
     x_own, x_peer, x_rows, y_raw, blocks, left, right, first, moved, acc,
-    scale_own, scale_far, part, far, passing,
-    own_sem, peram_sem, x_send, x_recv, y_send, y_recv, p_send, p_recv, s_send, s_recv, o_send, o_recv, r_send, r_recv,
+    scale_own, scale_far, part, far, passing, passing_blocks,
+    own_sem, peram_sem, x_send, x_recv, y_send, y_recv, p_send, p_recv, s_send, s_recv, o_send, o_recv, r_send, r_recv, b_send, b_recv,
 ):
     slices = lax.axis_size("tm")
     t, h = lax.axis_index("tm"), lax.axis_index("mode")
@@ -60,10 +60,10 @@
     relays = run // STRIDE
     share = span // relays
     rank = place // STRIDE
-    leads = [jnp.where(core == 1, 1 + 2 * q, STRIDE - 2 - 2 * q) for q in range(PIECES)]
+    lead = jnp.where(core == 1, 1, STRIDE - 2)
     at_source = place == jnp.where(core == 1, run - 1, 0)
     at_sink = place == jnp.where(core == 1, 1, run - 2)
-    relays_piece = [(lax.rem(place, STRIDE) == lead) & jnp.logical_not(at_sink) for lead in leads]
+    is_relay = (lax.rem(place, STRIDE) == lead) & jnp.logical_not(at_sink)
     sink = upper * run + jnp.where(core == 1, 1, run - 2)
     source = lax.rem(sink + jnp.where(core == 1, slices - 2, 2), slices)
     ahead = lax.rem(t + jnp.where(core == 1, 2, slices - 2), slices)
@@ -76,6 +76,14 @@
 
     def pass_on(q):
         return send(passing.at[q], y_raw.at[1, share_rows(q, rank)], r_send.at[q], y_recv.at[1, q], (sink, h))
+
+    held = slots // relays
+
+    def block_copy(k, dst, rsem, device):
+        return send(peram.at[0, pl.ds(k * held, held), 1], dst, p_send, rsem, device)
+
+    def pass_blocks():
+        return send(passing_blocks, blocks.at[1, pl.ds(rank * held, held)], b_send, p_recv, (sink, h))
 
     own_copy = pltpu.make_async_copy(elem.at[0], x_own, own_sem)
     own_copy.start()
@@ -94,14 +102,14 @@
     for device in near:
         pl.semaphore_signal(barrier, inc=1, device_id=device, device_id_type=MESH)
 
-    @pl.when(relays_piece[0] | relays_piece[1])
+    @pl.when(is_relay)
     def _():
         pl.semaphore_signal(barrier, inc=1, device_id=(source, h), device_id_type=MESH)
 
     @pl.when(at_sink)
     def _():
         def greet(n, _):
-            relay = upper * run + lax.rem(n, relays) * STRIDE + jnp.where(n < relays, leads[0], leads[1])
+            relay = upper * run + n * STRIDE + lead
 
             @pl.when(relay != t)
             def _():
@@ -109,23 +117,42 @@
 
             return 0
 
-        lax.fori_loop(0, PIECES * relays, greet, 0)
-
-    further = jnp.where(relays_piece[0] | relays_piece[1], 1, 0) + jnp.where(at_source, PIECES * relays - 1, 0)
+        lax.fori_loop(0, relays, greet, 0)
+
+    further = jnp.where(is_relay, 1, 0) + jnp.where(at_source, relays - 1, 0)
     pl.semaphore_wait(barrier, len(near) + further)
 
-    for i in range(2):
-        x_copy(i).start()
-
-    @pl.when(core == 1)
+    @pl.when(jnp.logical_not(at_source))
+    def _():
+        for i in range(2):
+            x_copy(i).start()
+
+    @pl.when((core == 1) & jnp.logical_not(at_source))
     def _():
         peram_copy().start()
+
+    @pl.when((core == 1) & at_source)
+    def _():
+        def spread_blocks(k, _):
+            relay = (1 - upper) * run + k * STRIDE + lead
+
+            @pl.when(relay == ahead)
+            def _():
+                block_copy(k, blocks.at[1, pl.ds(k * held, held)], p_recv, (relay, h)).start()
+
+            @pl.when(relay != ahead)
+            def _():
+                block_copy(k, passing_blocks, b_recv, (relay, h)).start()
+
+            return 0
+
+        lax.fori_loop(0, relays, spread_blocks, 0)
 
     @pl.when(at_source)
     def _():
         def spread(n, _):
             q, k = n // relays, lax.rem(n, relays)
-            relay = (1 - upper) * run + k * STRIDE + jnp.where(q == 0, leads[0], leads[1])
+            relay = (1 - upper) * run + k * STRIDE + lead
 
             @pl.when(relay == ahead)
             def _():
@@ -137,10 +164,13 @@
 
             return 0
 
-        group = relays // 2
-        for g in range(2 * PIECES):
-            lax.fori_loop(g * group, (g + 1) * group, spread, 0)
-            x_copy(2 + g).start()
+        lax.fori_loop(0, relays, spread, 0)
+        for g in range(2):
+            x_copy(g).start()
+        for g in range(2):
+            lax.fori_loop((2 + g) * relays // 2, (3 + g) * relays // 2, spread, 0)
+            x_copy(2 + 2 * g).start()
+            x_copy(3 + 2 * g).start()
 
     @pl.when(jnp.logical_not(at_source))
     def _():
@@ -191,6 +221,12 @@
         lay_rows(x_own[:, rows, :], i, own_rows)
         return 0
 
+    def relay_blocks():
+        @pl.when((core == 1) & is_relay)
+        def _():
+            block_copy(0, passing_blocks, b_recv, (source, h)).wait_recv()
+            pass_blocks().start()
+
     block_copies[0].wait()
     lay_blocks(0)
     own_copy.wait()
@@ -200,6 +236,8 @@
     def _():
         block_copies[1].wait()
 
+    relay_blocks()
+
     @pl.when(core == 1)
     def _():
         peram_copy().wait_recv()
@@ -217,7 +255,7 @@
             forward(q).start()
 
     def relay(q):
-        @pl.when(relays_piece[q])
+        @pl.when(is_relay)
         def _():
             share_copy(q, 0, passing.at[q], r_recv.at[q], (source, h)).wait_recv()
             pass_on(q).start()
@@ -348,10 +386,14 @@
         for q in range(PIECES):
             y_copy(0, q, (at(-1), h)).wait_send()
 
-    for q in range(PIECES):
-        @pl.when(relays_piece[q])
-        def _():
+    @pl.when(is_relay)
+    def _():
+        for q in range(PIECES):
             pass_on(q).wait_send()
+
+    @pl.when((core == 1) & is_relay)
+    def _():
+        pass_blocks().wait_send()
 
     for d in range(2):
         scale_copy(d).wait_send()
@@ -390,6 +432,7 @@
             pltpu.VMEM((2, slots, modes), F32),
             pltpu.VMEM((3, slots, modes), F32),
             pltpu.VMEM((PIECES, span * STRIDE * 2 // lax.axis_size("tm"), modes, modes), BF16),
+            pltpu.VMEM((slots * STRIDE * 2 // lax.axis_size("tm"), modes, modes), BF16),
             dma, dma((2,)),
             dma((chunks,)), dma((chunks,)),
             dma((2, PIECES)), dma((2, PIECES)),
@@ -397,6 +440,7 @@
             dma((2,)), dma((2,)),
             dma((3,)), dma((3,)),
             dma((PIECES,)), dma((PIECES,)),
+            dma, dma,
         ],
         compiler_params=pltpu.CompilerParams(
             collective_id=0, has_side_effects=True, vmem_limit_bytes=60 * 2**20

time: 76.4 us -> 75.2 us (0.984)
  the two profiles are of different devices: /device:TPU:229 before, /device:TPU:199 now
where the time goes in v3:
time: 75.2 us; the launch traced here: 75 us
  Pallas kernels  73.1 us (97%)
  local copies, waits for them, and re-layouts  1.32 us (2%)
    pallas_call x1, Pallas kernels, local(): pl.pallas_call(kernel, out_shape=jax.ShapeDtypeStruct((1, slots, 2), F32)...  73.1 us

profile of v3, /device:TPU:199, one launch (start us, length us, event | category | flops | bytes accessed | tf_op | source)
XLA Modules:
  0.0 75.0 jit_solution(11759011003058239649)
XLA Ops:
  0.7 73.1 %shard_map.46 = f32[1,8,2]{2,1,0:T(8,128)} custom-call(bf16[1,64,128,128]{3,2,1,0:T(8,128)(2,1)} %elem.1, f32[1]{0:T(128)S(6)} %copy.6.scale, s32[1,512]{1,0:T(1,128)} %bitcast.1, bf16[1,8,2,128,128]{4,3,2,1,0:T(8,128)(2,1)} %peram.1), custom_call_target="tpu_custom_call" | custom-call | tf_op jit(solution)/shard_map/pallas_call | solution.py:409
  73.7 1.3 %copy.5 = f32[1,8,2]{1,2,0:T(2,128)} copy(f32[1,8,2]{2,1,0:T(8,128)} %shard_map.46) | data formatting | bytes 128 | tf_op jit(solution)/shard_map/pallas_call | solution.py:409

commit v4 on v3

--- a/solution.py
+++ b/solution.py
@@ -264,8 +264,9 @@
         x_copy(i).wait_recv()
         lay_rows(x_peer[i], i, pl.multiple_of(other * half, half))
 
-    near_late = (core == 1) & at_source
-    far_late = (core == 1) & at_sink
+    near_late = (core == 1) & (at_source | (place == STRIDE - 1))
+    far_late = (core == 1) & (at_sink | (place == run - STRIDE + 1))
+    row_end = lax.rem(place, STRIDE) == STRIDE - 2
     early = chunks // 2
     last = PIECES - 1
 
@@ -284,7 +285,7 @@
             relay(last)
             take_chunk(3)
 
-        far_at = jnp.where(at_sink, jnp.where(core == 1, 3, 2), 1)
+        far_at = jnp.where(core == 1, jnp.where(far_late, 3, 2), jnp.where(row_end, 2, 1))
 
         @pl.when(n == far_at)
         def _():

time: 75.2 us -> 74.3 us (0.988)
  the two profiles are of different devices: /device:TPU:199 before, /device:TPU:1 now
where the time goes in v4:
time: 74.3 us; the launch traced here: 73.4 us
  Pallas kernels  71.4 us (96%)
  local copies, waits for them, and re-layouts  1.32 us (2%)
    pallas_call x1, Pallas kernels, local(): pl.pallas_call(kernel, out_shape=jax.ShapeDtypeStruct((1, slots, 2), F32)...  71.4 us

profile of v4, /device:TPU:1, one launch (start us, length us, event | category | flops | bytes accessed | tf_op | source)
XLA Modules:
  0.0 73.4 jit_solution(8032585238251647781)
XLA Ops:
  0.7 71.4 %shard_map.46 = f32[1,8,2]{2,1,0:T(8,128)} custom-call(bf16[1,64,128,128]{3,2,1,0:T(8,128)(2,1)} %elem.1, f32[1]{0:T(128)S(6)} %copy.6.scale, s32[1,512]{1,0:T(1,128)} %bitcast.1, bf16[1,8,2,128,128]{4,3,2,1,0:T(8,128)(2,1)} %peram.1), custom_call_target="tpu_custom_call" | custom-call | tf_op jit(solution)/shard_map/pallas_call | solution.py:410
  72.1 1.3 %copy.5 = f32[1,8,2]{1,2,0:T(2,128)} copy(f32[1,8,2]{2,1,0:T(8,128)} %shard_map.46) | data formatting | bytes 128 | tf_op jit(solution)/shard_map/pallas_call | solution.py:410

commit v5 on v4

--- a/solution.py
+++ b/solution.py
@@ -264,7 +264,7 @@
         x_copy(i).wait_recv()
         lay_rows(x_peer[i], i, pl.multiple_of(other * half, half))
 
-    near_late = (core == 1) & (at_source | (place == STRIDE - 1))
+    near_late = (core == 1) & (lax.rem(place, STRIDE) == STRIDE - 1)
     far_late = (core == 1) & (at_sink | (place == run - STRIDE + 1))
     row_end = lax.rem(place, STRIDE) == STRIDE - 2
     early = chunks // 2

time: 74.3 us -> 74.3 us (level)
  no operation moved by 1% of the time
where the time goes in v5:
time: 74.3 us; the launch traced here: 73.4 us
  Pallas kernels  71.4 us (96%)
  local copies, waits for them, and re-layouts  1.32 us (2%)
    pallas_call x1, Pallas kernels, local(): pl.pallas_call(kernel, out_shape=jax.ShapeDtypeStruct((1, slots, 2), F32)...  71.4 us

profile of v5, /device:TPU:1, one launch (start us, length us, event | category | flops | bytes accessed | tf_op | source)
XLA Modules:
  0.0 73.4 jit_solution(14390589406056724248)
XLA Ops:
  0.7 71.4 %shard_map.46 = f32[1,8,2]{2,1,0:T(8,128)} custom-call(bf16[1,64,128,128]{3,2,1,0:T(8,128)(2,1)} %elem.1, f32[1]{0:T(128)S(6)} %copy.6.scale, s32[1,512]{1,0:T(1,128)} %bitcast.1, bf16[1,8,2,128,128]{4,3,2,1,0:T(8,128)(2,1)} %peram.1), custom_call_target="tpu_custom_call" | custom-call | tf_op jit(solution)/shard_map/pallas_call | solution.py:410
  72.1 1.3 %copy.5 = f32[1,8,2]{1,2,0:T(2,128)} copy(f32[1,8,2]{2,1,0:T(8,128)} %shard_map.46) | data formatting | bytes 128 | tf_op jit(solution)/shard_map/pallas_call | solution.py:410
